TPU v7x, 32 devices: a whole 2x2x4 slice. The times are simulated.
32 devices in a mesh: parts: 2 (over x), ex: 16 (over z, y, core).
Axes of the slice: x: 2, y: 2, z: 4, core: 2. Of those that a mesh axis runs over, the one named last changes fastest.
Arguments:
- train_grads: float32 [2, 32768, 1024], P(None, ('parts', 'ex')), parts along dimension 1, may hold values from -300 to 300
- query_grads: float32 [2, 256, 1024], P(None, ('parts', 'ex')), parts along dimension 1, may hold values from -6 to 6
Outputs:
- scores: float32 [128, 32768], P(None, ('parts', 'ex')), parts along dimension 1
There are 2 independent parts, one for each index of `parts`. A program takes and returns all parts, laid end to end along the dimension named above; each array names one. Nothing has to cross between parts.
All inputs are finite; a program needn't handle non-finite values.
Results may differ from a plain program's by a relative error of at most 0.0003.
Values sent between devices are 32-bit elements; how exact they have to be, the bound alone decides.
A program may use at most 128 MiB of HBM per device.

v0:
```python
import jax
import jax.numpy as jnp
from jax import lax
from jax.sharding import PartitionSpec as P

ITERS = 12


DAMPING = 0.1


def chebyshev(rhs, hess, lower, upper):
    theta = (upper + lower) / 2.0
    delta = (upper - lower) / 2.0
    sigma = theta / delta

    def step(count, carry):
        solved, resid, direction, rho = carry
        solved = solved + direction
        resid = resid - jnp.dot(direction, hess, precision=lax.Precision.HIGHEST)
        rho_new = 1.0 / (2.0 * sigma - rho)
        direction = rho_new * rho * direction + 2.0 * rho_new / delta * resid
        return (solved, resid, direction, rho_new)

    start = (jnp.zeros_like(rhs), rhs, rhs / theta, (1.0 / sigma).astype(jnp.float32))
    return lax.fori_loop(0, ITERS, step, start)[0]


def precondition(queries, gram, total_rows):
    width = gram.shape[0]
    damping = DAMPING * jnp.trace(gram) / (total_rows * width)
    hess = gram / total_rows + damping * jnp.eye(width, dtype=jnp.float32)
    upper = jnp.max(jnp.sum(jnp.abs(hess), axis=1))
    return chebyshev(queries, hess, damping, upper)


def shards(train_grads, query_grads):
    layers_count = train_grads.shape[0]
    width = train_grads.shape[2]
    total_rows = train_grads.shape[1] * lax.axis_size("ex")
    payloads = []
    for layer in range(layers_count):
        grads = train_grads[layer]
        partial_gram = jnp.einsum("nk,nj->kj", grads, grads, precision=lax.Precision.HIGHEST)
        payloads.append(partial_gram)
    summed = []
    for layer in range(layers_count):
        summed.append(lax.psum(payloads[layer], "ex"))
    results = []
    for layer in range(layers_count):
        gram = summed[layer]
        results.append(precondition(query_grads[layer], gram, total_rows))
    stacked = jnp.stack(results)
    score_scale = 1.0 / width**0.5
    return (
        jnp.einsum(
            "lrk,lnk->rn",
            lax.all_gather(stacked, "ex", axis=1, tiled=True),
            train_grads,
            precision=lax.Precision.HIGHEST,
        )
        * score_scale
    )


def solution(mesh):
    in_specs = (P(None, ("parts", "ex"), None), P(None, ("parts", "ex"), None))
    out_specs = P(None, ("parts", "ex"))
    return jax.shard_map(shards, mesh=mesh, in_specs=in_specs, out_specs=out_specs, check_vma=False)
```

profile of v0, /device:TPU:27, one launch (start us, length us, event | category | flops | bytes accessed | tf_op | source)
XLA Modules:
  0.0 390.4 jit_solution(6066567746688797122)
XLA Ops:
  6.5 17.7 %fusion = f32[1024,1024]{1,0:T(8,128)} fusion(f32[2,1024,1024]{2,1,0:T(8,128)} %param.6), kind=kOutput, calls=%fused_computation.6 | convolution fusion | flops 12884901888 | bytes 8388608 | tf_op jit(solution)/shard_map/nk,nj->kj/dot_general | solution.py:44
  24.3 14.8 %fusion.2 = f32[1024,1024]{1,0:T(8,128)} fusion(f32[2,1024,1024]{2,1,0:T(8,128)S(1)} %copy-done.1), kind=kOutput, calls=%fused_computation.8 | convolution fusion | flops 12884901888 | bytes 8388608 | tf_op jit(solution)/shard_map/nk,nj->kj/dot_general | solution.py:44
  39.9 169.6 %all-reduce.3.cloned.1.call-done = (f32[1024,1024]{1,0:T(8,128)}, f32[1024,1024]{1,0:T(8,128)}) async-done(((f32[1024,1024]{1,0:T(8,128)}, f32[1024,1024]{1,0:T(8,128)}), (f32[1024,1024]{1,0:T(8,128)}, f32[1024,1024]{1,0:T(8,128)})) %all-reduce.3.cloned.1.call-update) | async-done | bytes 8388624 | tf_op jit(solution)/shard_map/psum | solution.py:48
  215.0 7.2 %abs_reduce_fusion = (f32[1024]{0:T(1024)S(1)}, f32[1024,1024]{1,0:T(8,128)}, f32[1024]{0:T(1024)S(1)}, f32[1024,1024]{1,0:T(8,128)}) fusion(f32[]{:T(128)S(6)} %div.77, f32[1024,1024]{1,0:T(8,128)} %get-tuple-element.281, f32[]{:T(128)S(6)} %div.69, f32[1024,1024]{1,0:T(8,128)} %get-tuple-element.282), kind=kLoop, calls=%fused_computation.10 | loop fusion | flops 11532288 | bytes 16785416 | tf_op jit(solution)/shard_map/reduce_sum | solution.py:33
  226.0 52.8 %while.38 = (s32[]{:T(128)}, f32[8,1024]{1,0:T(8,128)S(1)}, f32[8,1024]{1,0:T(8,128)S(1)}, f32[8,1024]{1,0:T(8,128)S(1)}, f32[]{:T(128)}, /*index=5*/f32[1024,10...) while((s32[]{:T(128)}, f32[8,1024]{1,0:T(8,128)S(1)}, ...), condition=%wide.region_5.6_spmd.clone, body=%wide.region_4.5_spmd.clone.sunk | while | flops 100712456 | bytes 4456651 | solution.py:26
  226.3 4.3 %multiply_add_fusion.4 = (f32[8,1024]{1,0:T(8,128)S(1)}, f32[8,1024]{1,0:T(8,128)S(1)}, f32[8,1024]{1,0:T(8,128)S(1)}) fusion(f32[8,1024]{1,0:T(8,128)S(1)} %copy.37, f32[]{:T(128)S(6)} %div.101, f32[]{:T(128)S(6)} %mul.145, f32[8,1024]{1,0:T(8,128)S(1)} %get-tuple-element.458, pred[]{:T(512)S(6)} %compare.6, f32[8,1024]{1,0:T(8,128)S(1)} %get-tuple-element.459, ...), kind=kOutput, calls=%fused_computation.2.clone.1 | convolution fusion | flops 100712448 | bytes 4390921 | tf_op jit(solution)/shard_map/while/body/eval_jaxpr/dot_general | solution.py:20
  230.7 4.3 %multiply_add_fusion.4 = (f32[8,1024]{1,0:T(8,128)S(1)}, f32[8,1024]{1,0:T(8,128)S(1)}, f32[8,1024]{1,0:T(8,128)S(1)}) fusion(f32[8,1024]{1,0:T(8,128)S(1)} %copy.37, f32[]{:T(128)S(6)} %div.101, f32[]{:T(128)S(6)} %mul.145, f32[8,1024]{1,0:T(8,128)S(1)} %get-tuple-element.458, pred[]{:T(512)S(6)} %compare.6, f32[8,1024]{1,0:T(8,128)S(1)} %get-tuple-element.459, ...), kind=kOutput, calls=%fused_computation.2.clone.1 | convolution fusion | flops 100712448 | bytes 4390921 | tf_op jit(solution)/shard_map/while/body/eval_jaxpr/dot_general | solution.py:20
  235.1 4.3 %multiply_add_fusion.4 = (f32[8,1024]{1,0:T(8,128)S(1)}, f32[8,1024]{1,0:T(8,128)S(1)}, f32[8,1024]{1,0:T(8,128)S(1)}) fusion(f32[8,1024]{1,0:T(8,128)S(1)} %copy.37, f32[]{:T(128)S(6)} %div.101, f32[]{:T(128)S(6)} %mul.145, f32[8,1024]{1,0:T(8,128)S(1)} %get-tuple-element.458, pred[]{:T(512)S(6)} %compare.6, f32[8,1024]{1,0:T(8,128)S(1)} %get-tuple-element.459, ...), kind=kOutput, calls=%fused_computation.2.clone.1 | convolution fusion | flops 100712448 | bytes 4390921 | tf_op jit(solution)/shard_map/while/body/eval_jaxpr/dot_general | solution.py:20
  239.5 4.3 %multiply_add_fusion.4 = (f32[8,1024]{1,0:T(8,128)S(1)}, f32[8,1024]{1,0:T(8,128)S(1)}, f32[8,1024]{1,0:T(8,128)S(1)}) fusion(f32[8,1024]{1,0:T(8,128)S(1)} %copy.37, f32[]{:T(128)S(6)} %div.101, f32[]{:T(128)S(6)} %mul.145, f32[8,1024]{1,0:T(8,128)S(1)} %get-tuple-element.458, pred[]{:T(512)S(6)} %compare.6, f32[8,1024]{1,0:T(8,128)S(1)} %get-tuple-element.459, ...), kind=kOutput, calls=%fused_computation.2.clone.1 | convolution fusion | flops 100712448 | bytes 4390921 | tf_op jit(solution)/shard_map/while/body/eval_jaxpr/dot_general | solution.py:20
  243.9 4.3 %multiply_add_fusion.4 = (f32[8,1024]{1,0:T(8,128)S(1)}, f32[8,1024]{1,0:T(8,128)S(1)}, f32[8,1024]{1,0:T(8,128)S(1)}) fusion(f32[8,1024]{1,0:T(8,128)S(1)} %copy.37, f32[]{:T(128)S(6)} %div.101, f32[]{:T(128)S(6)} %mul.145, f32[8,1024]{1,0:T(8,128)S(1)} %get-tuple-element.458, pred[]{:T(512)S(6)} %compare.6, f32[8,1024]{1,0:T(8,128)S(1)} %get-tuple-element.459, ...), kind=kOutput, calls=%fused_computation.2.clone.1 | convolution fusion | flops 100712448 | bytes 4390921 | tf_op jit(solution)/shard_map/while/body/eval_jaxpr/dot_general | solution.py:20
  248.3 4.3 %multiply_add_fusion.4 = (f32[8,1024]{1,0:T(8,128)S(1)}, f32[8,1024]{1,0:T(8,128)S(1)}, f32[8,1024]{1,0:T(8,128)S(1)}) fusion(f32[8,1024]{1,0:T(8,128)S(1)} %copy.37, f32[]{:T(128)S(6)} %div.101, f32[]{:T(128)S(6)} %mul.145, f32[8,1024]{1,0:T(8,128)S(1)} %get-tuple-element.458, pred[]{:T(512)S(6)} %compare.6, f32[8,1024]{1,0:T(8,128)S(1)} %get-tuple-element.459, ...), kind=kOutput, calls=%fused_computation.2.clone.1 | convolution fusion | flops 100712448 | bytes 4390921 | tf_op jit(solution)/shard_map/while/body/eval_jaxpr/dot_general | solution.py:20
  252.6 4.3 %multiply_add_fusion.4 = (f32[8,1024]{1,0:T(8,128)S(1)}, f32[8,1024]{1,0:T(8,128)S(1)}, f32[8,1024]{1,0:T(8,128)S(1)}) fusion(f32[8,1024]{1,0:T(8,128)S(1)} %copy.37, f32[]{:T(128)S(6)} %div.101, f32[]{:T(128)S(6)} %mul.145, f32[8,1024]{1,0:T(8,128)S(1)} %get-tuple-element.458, pred[]{:T(512)S(6)} %compare.6, f32[8,1024]{1,0:T(8,128)S(1)} %get-tuple-element.459, ...), kind=kOutput, calls=%fused_computation.2.clone.1 | convolution fusion | flops 100712448 | bytes 4390921 | tf_op jit(solution)/shard_map/while/body/eval_jaxpr/dot_general | solution.py:20
  257.0 4.3 %multiply_add_fusion.4 = (f32[8,1024]{1,0:T(8,128)S(1)}, f32[8,1024]{1,0:T(8,128)S(1)}, f32[8,1024]{1,0:T(8,128)S(1)}) fusion(f32[8,1024]{1,0:T(8,128)S(1)} %copy.37, f32[]{:T(128)S(6)} %div.101, f32[]{:T(128)S(6)} %mul.145, f32[8,1024]{1,0:T(8,128)S(1)} %get-tuple-element.458, pred[]{:T(512)S(6)} %compare.6, f32[8,1024]{1,0:T(8,128)S(1)} %get-tuple-element.459, ...), kind=kOutput, calls=%fused_computation.2.clone.1 | convolution fusion | flops 100712448 | bytes 4390921 | tf_op jit(solution)/shard_map/while/body/eval_jaxpr/dot_general | solution.py:20
  261.4 4.3 %multiply_add_fusion.4 = (f32[8,1024]{1,0:T(8,128)S(1)}, f32[8,1024]{1,0:T(8,128)S(1)}, f32[8,1024]{1,0:T(8,128)S(1)}) fusion(f32[8,1024]{1,0:T(8,128)S(1)} %copy.37, f32[]{:T(128)S(6)} %div.101, f32[]{:T(128)S(6)} %mul.145, f32[8,1024]{1,0:T(8,128)S(1)} %get-tuple-element.458, pred[]{:T(512)S(6)} %compare.6, f32[8,1024]{1,0:T(8,128)S(1)} %get-tuple-element.459, ...), kind=kOutput, calls=%fused_computation.2.clone.1 | convolution fusion | flops 100712448 | bytes 4390921 | tf_op jit(solution)/shard_map/while/body/eval_jaxpr/dot_general | solution.py:20
  265.8 4.3 %multiply_add_fusion.4 = (f32[8,1024]{1,0:T(8,128)S(1)}, f32[8,1024]{1,0:T(8,128)S(1)}, f32[8,1024]{1,0:T(8,128)S(1)}) fusion(f32[8,1024]{1,0:T(8,128)S(1)} %copy.37, f32[]{:T(128)S(6)} %div.101, f32[]{:T(128)S(6)} %mul.145, f32[8,1024]{1,0:T(8,128)S(1)} %get-tuple-element.458, pred[]{:T(512)S(6)} %compare.6, f32[8,1024]{1,0:T(8,128)S(1)} %get-tuple-element.459, ...), kind=kOutput, calls=%fused_computation.2.clone.1 | convolution fusion | flops 100712448 | bytes 4390921 | tf_op jit(solution)/shard_map/while/body/eval_jaxpr/dot_general | solution.py:20
  270.2 4.3 %multiply_add_fusion.4 = (f32[8,1024]{1,0:T(8,128)S(1)}, f32[8,1024]{1,0:T(8,128)S(1)}, f32[8,1024]{1,0:T(8,128)S(1)}) fusion(f32[8,1024]{1,0:T(8,128)S(1)} %copy.37, f32[]{:T(128)S(6)} %div.101, f32[]{:T(128)S(6)} %mul.145, f32[8,1024]{1,0:T(8,128)S(1)} %get-tuple-element.458, pred[]{:T(512)S(6)} %compare.6, f32[8,1024]{1,0:T(8,128)S(1)} %get-tuple-element.459, ...), kind=kOutput, calls=%fused_computation.2.clone.1 | convolution fusion | flops 100712448 | bytes 4390921 | tf_op jit(solution)/shard_map/while/body/eval_jaxpr/dot_general | solution.py:20
  274.6 4.3 %multiply_add_fusion.4 = (f32[8,1024]{1,0:T(8,128)S(1)}, f32[8,1024]{1,0:T(8,128)S(1)}, f32[8,1024]{1,0:T(8,128)S(1)}) fusion(f32[8,1024]{1,0:T(8,128)S(1)} %copy.37, f32[]{:T(128)S(6)} %div.101, f32[]{:T(128)S(6)} %mul.145, f32[8,1024]{1,0:T(8,128)S(1)} %get-tuple-element.458, pred[]{:T(512)S(6)} %compare.6, f32[8,1024]{1,0:T(8,128)S(1)} %get-tuple-element.459, ...), kind=kOutput, calls=%fused_computation.2.clone.1 | convolution fusion | flops 100712448 | bytes 4390921 | tf_op jit(solution)/shard_map/while/body/eval_jaxpr/dot_general | solution.py:20
  278.8 52.6 %while.39 = (s32[]{:T(128)}, f32[8,1024]{1,0:T(8,128)S(1)}, f32[8,1024]{1,0:T(8,128)S(1)}, f32[8,1024]{1,0:T(8,128)S(1)}, f32[]{:T(128)}, /*index=5*/f32[1024,10...) while((s32[]{:T(128)}, f32[8,1024]{1,0:T(8,128)S(1)}, ...), condition=%wide.region_11.12_spmd.clone, body=%wide.region_10.11_spmd.clone.sunk | while | flops 100712456 | bytes 4456651 | solution.py:26
  278.9 4.3 %multiply_add_fusion.5 = (f32[8,1024]{1,0:T(8,128)S(1)}, f32[8,1024]{1,0:T(8,128)S(1)}, f32[8,1024]{1,0:T(8,128)S(1)}) fusion(f32[8,1024]{1,0:T(8,128)S(1)} %copy.38, f32[]{:T(128)S(6)} %div.103, f32[]{:T(128)S(6)} %mul.151, f32[8,1024]{1,0:T(8,128)S(1)} %get-tuple-element.422, pred[]{:T(512)S(6)} %compare.7, f32[8,1024]{1,0:T(8,128)S(1)} %get-tuple-element.423, ...), kind=kOutput, calls=%fused_computation.5.clone.1 | convolution fusion | flops 100712448 | bytes 4390921 | tf_op jit(solution)/shard_map/while/body/eval_jaxpr/dot_general | solution.py:20
  283.3 4.3 %multiply_add_fusion.5 = (f32[8,1024]{1,0:T(8,128)S(1)}, f32[8,1024]{1,0:T(8,128)S(1)}, f32[8,1024]{1,0:T(8,128)S(1)}) fusion(f32[8,1024]{1,0:T(8,128)S(1)} %copy.38, f32[]{:T(128)S(6)} %div.103, f32[]{:T(128)S(6)} %mul.151, f32[8,1024]{1,0:T(8,128)S(1)} %get-tuple-element.422, pred[]{:T(512)S(6)} %compare.7, f32[8,1024]{1,0:T(8,128)S(1)} %get-tuple-element.423, ...), kind=kOutput, calls=%fused_computation.5.clone.1 | convolution fusion | flops 100712448 | bytes 4390921 | tf_op jit(solution)/shard_map/while/body/eval_jaxpr/dot_general | solution.py:20
  287.7 4.3 %multiply_add_fusion.5 = (f32[8,1024]{1,0:T(8,128)S(1)}, f32[8,1024]{1,0:T(8,128)S(1)}, f32[8,1024]{1,0:T(8,128)S(1)}) fusion(f32[8,1024]{1,0:T(8,128)S(1)} %copy.38, f32[]{:T(128)S(6)} %div.103, f32[]{:T(128)S(6)} %mul.151, f32[8,1024]{1,0:T(8,128)S(1)} %get-tuple-element.422, pred[]{:T(512)S(6)} %compare.7, f32[8,1024]{1,0:T(8,128)S(1)} %get-tuple-element.423, ...), kind=kOutput, calls=%fused_computation.5.clone.1 | convolution fusion | flops 100712448 | bytes 4390921 | tf_op jit(solution)/shard_map/while/body/eval_jaxpr/dot_general | solution.py:20
  292.1 4.3 %multiply_add_fusion.5 = (f32[8,1024]{1,0:T(8,128)S(1)}, f32[8,1024]{1,0:T(8,128)S(1)}, f32[8,1024]{1,0:T(8,128)S(1)}) fusion(f32[8,1024]{1,0:T(8,128)S(1)} %copy.38, f32[]{:T(128)S(6)} %div.103, f32[]{:T(128)S(6)} %mul.151, f32[8,1024]{1,0:T(8,128)S(1)} %get-tuple-element.422, pred[]{:T(512)S(6)} %compare.7, f32[8,1024]{1,0:T(8,128)S(1)} %get-tuple-element.423, ...), kind=kOutput, calls=%fused_computation.5.clone.1 | convolution fusion | flops 100712448 | bytes 4390921 | tf_op jit(solution)/shard_map/while/body/eval_jaxpr/dot_general | solution.py:20
  296.5 4.3 %multiply_add_fusion.5 = (f32[8,1024]{1,0:T(8,128)S(1)}, f32[8,1024]{1,0:T(8,128)S(1)}, f32[8,1024]{1,0:T(8,128)S(1)}) fusion(f32[8,1024]{1,0:T(8,128)S(1)} %copy.38, f32[]{:T(128)S(6)} %div.103, f32[]{:T(128)S(6)} %mul.151, f32[8,1024]{1,0:T(8,128)S(1)} %get-tuple-element.422, pred[]{:T(512)S(6)} %compare.7, f32[8,1024]{1,0:T(8,128)S(1)} %get-tuple-element.423, ...), kind=kOutput, calls=%fused_computation.5.clone.1 | convolution fusion | flops 100712448 | bytes 4390921 | tf_op jit(solution)/shard_map/while/body/eval_jaxpr/dot_general | solution.py:20
  300.9 4.3 %multiply_add_fusion.5 = (f32[8,1024]{1,0:T(8,128)S(1)}, f32[8,1024]{1,0:T(8,128)S(1)}, f32[8,1024]{1,0:T(8,128)S(1)}) fusion(f32[8,1024]{1,0:T(8,128)S(1)} %copy.38, f32[]{:T(128)S(6)} %div.103, f32[]{:T(128)S(6)} %mul.151, f32[8,1024]{1,0:T(8,128)S(1)} %get-tuple-element.422, pred[]{:T(512)S(6)} %compare.7, f32[8,1024]{1,0:T(8,128)S(1)} %get-tuple-element.423, ...), kind=kOutput, calls=%fused_computation.5.clone.1 | convolution fusion | flops 100712448 | bytes 4390921 | tf_op jit(solution)/shard_map/while/body/eval_jaxpr/dot_general | solution.py:20
  305.2 4.3 %multiply_add_fusion.5 = (f32[8,1024]{1,0:T(8,128)S(1)}, f32[8,1024]{1,0:T(8,128)S(1)}, f32[8,1024]{1,0:T(8,128)S(1)}) fusion(f32[8,1024]{1,0:T(8,128)S(1)} %copy.38, f32[]{:T(128)S(6)} %div.103, f32[]{:T(128)S(6)} %mul.151, f32[8,1024]{1,0:T(8,128)S(1)} %get-tuple-element.422, pred[]{:T(512)S(6)} %compare.7, f32[8,1024]{1,0:T(8,128)S(1)} %get-tuple-element.423, ...), kind=kOutput, calls=%fused_computation.5.clone.1 | convolution fusion | flops 100712448 | bytes 4390921 | tf_op jit(solution)/shard_map/while/body/eval_jaxpr/dot_general | solution.py:20
  309.6 4.3 %multiply_add_fusion.5 = (f32[8,1024]{1,0:T(8,128)S(1)}, f32[8,1024]{1,0:T(8,128)S(1)}, f32[8,1024]{1,0:T(8,128)S(1)}) fusion(f32[8,1024]{1,0:T(8,128)S(1)} %copy.38, f32[]{:T(128)S(6)} %div.103, f32[]{:T(128)S(6)} %mul.151, f32[8,1024]{1,0:T(8,128)S(1)} %get-tuple-element.422, pred[]{:T(512)S(6)} %compare.7, f32[8,1024]{1,0:T(8,128)S(1)} %get-tuple-element.423, ...), kind=kOutput, calls=%fused_computation.5.clone.1 | convolution fusion | flops 100712448 | bytes 4390921 | tf_op jit(solution)/shard_map/while/body/eval_jaxpr/dot_general | solution.py:20
  314.0 4.3 %multiply_add_fusion.5 = (f32[8,1024]{1,0:T(8,128)S(1)}, f32[8,1024]{1,0:T(8,128)S(1)}, f32[8,1024]{1,0:T(8,128)S(1)}) fusion(f32[8,1024]{1,0:T(8,128)S(1)} %copy.38, f32[]{:T(128)S(6)} %div.103, f32[]{:T(128)S(6)} %mul.151, f32[8,1024]{1,0:T(8,128)S(1)} %get-tuple-element.422, pred[]{:T(512)S(6)} %compare.7, f32[8,1024]{1,0:T(8,128)S(1)} %get-tuple-element.423, ...), kind=kOutput, calls=%fused_computation.5.clone.1 | convolution fusion | flops 100712448 | bytes 4390921 | tf_op jit(solution)/shard_map/while/body/eval_jaxpr/dot_general | solution.py:20
  318.4 4.3 %multiply_add_fusion.5 = (f32[8,1024]{1,0:T(8,128)S(1)}, f32[8,1024]{1,0:T(8,128)S(1)}, f32[8,1024]{1,0:T(8,128)S(1)}) fusion(f32[8,1024]{1,0:T(8,128)S(1)} %copy.38, f32[]{:T(128)S(6)} %div.103, f32[]{:T(128)S(6)} %mul.151, f32[8,1024]{1,0:T(8,128)S(1)} %get-tuple-element.422, pred[]{:T(512)S(6)} %compare.7, f32[8,1024]{1,0:T(8,128)S(1)} %get-tuple-element.423, ...), kind=kOutput, calls=%fused_computation.5.clone.1 | convolution fusion | flops 100712448 | bytes 4390921 | tf_op jit(solution)/shard_map/while/body/eval_jaxpr/dot_general | solution.py:20
  322.8 4.3 %multiply_add_fusion.5 = (f32[8,1024]{1,0:T(8,128)S(1)}, f32[8,1024]{1,0:T(8,128)S(1)}, f32[8,1024]{1,0:T(8,128)S(1)}) fusion(f32[8,1024]{1,0:T(8,128)S(1)} %copy.38, f32[]{:T(128)S(6)} %div.103, f32[]{:T(128)S(6)} %mul.151, f32[8,1024]{1,0:T(8,128)S(1)} %get-tuple-element.422, pred[]{:T(512)S(6)} %compare.7, f32[8,1024]{1,0:T(8,128)S(1)} %get-tuple-element.423, ...), kind=kOutput, calls=%fused_computation.5.clone.1 | convolution fusion | flops 100712448 | bytes 4390921 | tf_op jit(solution)/shard_map/while/body/eval_jaxpr/dot_general | solution.py:20
  327.2 4.3 %multiply_add_fusion.5 = (f32[8,1024]{1,0:T(8,128)S(1)}, f32[8,1024]{1,0:T(8,128)S(1)}, f32[8,1024]{1,0:T(8,128)S(1)}) fusion(f32[8,1024]{1,0:T(8,128)S(1)} %copy.38, f32[]{:T(128)S(6)} %div.103, f32[]{:T(128)S(6)} %mul.151, f32[8,1024]{1,0:T(8,128)S(1)} %get-tuple-element.422, pred[]{:T(512)S(6)} %compare.7, f32[8,1024]{1,0:T(8,128)S(1)} %get-tuple-element.423, ...), kind=kOutput, calls=%fused_computation.5.clone.1 | convolution fusion | flops 100712448 | bytes 4390921 | tf_op jit(solution)/shard_map/while/body/eval_jaxpr/dot_general | solution.py:20
  332.1 38.3 %all-gather.2.cloned.1.call-done = f32[2,128,1024]{2,1,0:T(8,128)} async-done(((f32[2,8,1024]{2,1,0:T(8,128)}), f32[2,128,1024]{2,1,0:T(8,128)}) %all-gather.2.cloned.1.call-update) | async-done | bytes 1048592 | tf_op jit(solution)/shard_map/all_gather | solution.py:58
  370.4 13.2 %fusion.6 = f32[128,1024]{1,0:T(8,128)} fusion(f32[2,128,1024]{2,1,0:T(8,128)} %all-gather.2.cloned.1.call-done, f32[2,1024,1024]{2,1,0:T(8,128)} %param.6), kind=kOutput, calls=%fused_computation.20 | convolution fusion | flops 3221356544 | bytes 9961472 | tf_op jit(solution)/shard_map/lrk,lnk->rn/dot_general | solution.py:56
  (43 shorter events, 7.0 us)
Async XLA Ops:
  6.5 202.9 %all-reduce.3.cloned.1.call-start = ((), (), s32[]{:S(2)}) async-start(), calls=%async_computation.1 | async-start | bytes 16777216 | tf_op jit(solution)/shard_map/psum | solution.py:48
  6.5 17.7 %copy-start.1 = (f32[2,1024,1024]{2,1,0:T(8,128)S(1)}, f32[2,1024,1024]{2,1,0:T(8,128)}, u32[]{:S(2)}) copy-start(f32[2,1024,1024]{2,1,0:T(8,128)} %param.6) | copy-start | bytes 25165828
  39.0 0.8 copy-start.2
  39.1 331.3 %all-gather.2.cloned.1.call-start = ((), (), s32[]{:S(2)}) async-start(), calls=%async_computation | async-start | bytes 1114112 | tf_op jit(solution)/shard_map/all_gather | solution.py:58
  209.5 3.4 copy-start
Sparse Core Ops, SparseCore 0:
  39.2 170.2 all-reduce.2
  332.2 38.1 all-gather.1
where the time goes:
time: 394 us; the launch traced here: 390 us
  waiting for transfers between devices  208 us (53%)
  matrix products  148 us (38%)
  between operations  17.3 us (4%)
  other arithmetic  13 us (3%)
    psum x1, waiting for transfers between devices, shards(): summed.append(lax.psum(payloads[layer], 'ex'))  170 us
    dot_general x24, matrix products, step(): resid = resid - jnp.dot(direction, hess, precision=lax.Precision.HIGHEST)  103 us
    all_gather x1, waiting for transfers between devices, shards(): lax.all_gather(stacked, 'ex', axis=1, tiled=True)  38.3 us
    dot_general x2, matrix products, shards(): jnp.einsum('nk,nj->kj', grads, grads, precision=lax.Precision.HIGHEST)  32.5 us
    dot_general x1, matrix products, shards(): jnp.einsum('lrk,lnk->rn', lax.all_gather(stacked, 'ex', axis=1, tiled=Tru...  13.2 us
  transfers between devices with their start and end apart: 2, of which 2 were waited for; matrix products, arithmetic and copies ran while one was open for 0% of the time, Pallas kernels for 0%

commit v1 on v0

v1 whole, which is shorter than its diff:
```python
import functools

import jax
import jax.numpy as jnp
from jax import lax
from jax.experimental import pallas as pl
from jax.experimental.pallas import tpu as pltpu
from jax.sharding import PartitionSpec as P

ITERS = 12
DAMPING = 0.1
TILE = 128
SPLIT = 4
PIECES = 4

F32 = jnp.float32
BF16 = jnp.bfloat16


def halves(value):
    high = value.astype(BF16)
    return high, (value - high.astype(F32)).astype(BF16)


def dot(left, right, dims):
    return lax.dot_general(left, right, (dims, ((), ())), preferred_element_type=F32)


def remote(src, dst, send, recv, target):
    return pltpu.make_async_remote_copy(
        src_ref=src,
        dst_ref=dst,
        send_sem=send,
        recv_sem=recv,
        device_id={"ex": target},
        device_id_type=pl.DeviceIdType.MESH,
    )


def kernel(
    n, train, query, out,
    rows_f32, high, low, part, acc, sib_buf, y_buf, left_buf, right_buf, full,
    hess, hess_high, hess_low, solved_all, rhs, direction, stacked,
    load_sem, q_send, q_recv, q_local, sib_send, sib_recv, y_send, y_recv, z_send, left_recv, right_recv,
    full_send, full_recv, bz_send, by_send, bs_send, bz_recv, by_recv, bs_recv,
):
    layers, rows, width = train.shape
    depth = query.shape[1]
    strips = width // TILE
    pairs = strips // 2
    mine = pairs // 2
    piece = TILE // SPLIT
    total_rows = rows * n
    half = depth * n // 2
    step_rows = half // PIECES
    chips = n // 4
    root = (chips - 1) // 2

    me = lax.axis_index("ex")
    core = lax.rem(me, 2)
    y = lax.rem(me // 2, 2)
    z = me // 4
    sibling = me + 1 - 2 * core
    across = me + 2 - 4 * y
    is_root = z == root
    my_half = me // (n // 2)
    my_slot = lax.rem(me, n // 2)

    def layer_at(turn):
        return jnp.where(turn == 0, 1 - y, y)

    def load(turn):
        layer = layer_at(turn)
        return pltpu.make_async_copy(train.at[layer], rows_f32.at[turn], load_sem.at[turn])

    load(0).start()
    load(1).start()

    barrier = pltpu.get_barrier_semaphore()

    def greet(j, _):
        pl.semaphore_signal(
            barrier, inc=1, device_id={"ex": lax.rem(me + j, n)}, device_id_type=pl.DeviceIdType.MESH
        )
        return 0

    lax.fori_loop(1, n, greet, 0)
    pl.semaphore_wait(barrier, n - 1)

    def query_copy(layer):
        target = root * 4 + layer * 2 + my_half
        slot = rhs.at[pl.ds(pl.multiple_of(my_slot * depth, 8), depth)]
        return target, query.at[layer], slot

    for layer in range(layers):
        target, src, slot = query_copy(layer)

        @pl.when(target != me)
        def _():
            remote(src, slot, q_send.at[layer], q_recv.at[my_slot], target).start()

        @pl.when(target == me)
        def _():
            pltpu.make_async_copy(src, slot, q_local).start()

    def sib_copy(turn, k):
        return remote(
            part.at[turn, 2 * k + 1 - core], sib_buf.at[turn, k],
            sib_send.at[turn, k], sib_recv.at[turn, k], sibling,
        )

    def y_copy(k, s):
        sl = pl.ds(s * piece, piece)
        return remote(acc.at[0, k, sl], y_buf.at[k, sl], y_send.at[k, s], y_recv.at[k, s], across)

    def left_copy(k, s):
        sl = pl.ds(s * piece, piece)
        return remote(acc.at[1, k, sl], left_buf.at[k, sl], z_send.at[k, s], left_recv.at[k, s], me + 4)

    def right_copy(k, s):
        sl = pl.ds(s * piece, piece)
        return remote(acc.at[1, k, sl], right_buf.at[k, sl], z_send.at[k, s], right_recv.at[k, s], me - 4)

    def full_copy(k, s):
        src = full.at[2 * k + core, pl.ds(s * piece, piece)]
        return remote(src, src, full_send.at[k, s], full_recv.at[k, s], sibling)

    def full_wait(k, s):
        src = full.at[2 * k + 1 - core, pl.ds(s * piece, piece)]
        remote(src, src, full_send.at[k, s], full_recv.at[k, s], sibling).wait_recv()

    def merge(turn, k):
        sib_copy(turn, k).wait_recv()
        acc[turn, k] = part[turn, 2 * k + core] + sib_buf[turn, k]

        @pl.when(turn == 0)
        def _():
            for s in range(SPLIT):
                y_copy(k, s).start()

    def gram(turn, _):
        load(turn).wait()

        def cut(b, _):
            sl = pl.ds(pl.multiple_of(b * TILE, TILE), TILE)
            high[turn, sl], low[turn, sl] = halves(rows_f32[turn, sl])
            return 0

        lax.fori_loop(0, rows // TILE, cut, 0)
        for p in range(pairs):
            column = 0
            for i in (p, strips - 1 - p):
                span = (strips - i) * TILE
                lo, hi = i * TILE, (i + 1) * TILE
                left_high = high[turn, :, lo:hi]
                left_low = low[turn, :, lo:hi]
                right_high = high[turn, :, lo:]
                right_low = low[turn, :, lo:]
                dims = ((0,), (0,))
                part[turn, p, :, column:column + span] = (
                    dot(left_high, right_low, dims) + dot(left_low, right_high, dims)
                ) + dot(left_high, right_high, dims)
                column += span

            @pl.when(core != p % 2)
            def _():
                sib_copy(turn, p // 2).start()

            if p >= 2 and p % 2 == 0:
                merge(turn, p // 2 - 1)
        merge(turn, mine - 1)
        return 0

    lax.fori_loop(0, 2, gram, 0)

    from_left = jnp.logical_and(z > 0, z <= root)
    from_right = jnp.logical_and(z < chips - 1, z >= root)
    for k in range(mine):
        for s in range(SPLIT):
            sl = pl.ds(s * piece, piece)
            y_copy(k, s).wait_recv()
            acc[1, k, sl] = acc[1, k, sl] + y_buf[k, sl]

            @pl.when(from_left)
            def _():
                left_copy(k, s).wait_recv()
                acc[1, k, sl] = acc[1, k, sl] + left_buf[k, sl]

            @pl.when(from_right)
            def _():
                right_copy(k, s).wait_recv()
                acc[1, k, sl] = acc[1, k, sl] + right_buf[k, sl]

            @pl.when(z < root)
            def _():
                left_copy(k, s).start()

            @pl.when(z > root)
            def _():
                right_copy(k, s).start()

            @pl.when(is_root)
            def _():
                full[2 * k + core, sl] = acc[1, k, sl]
                full_copy(k, s).start()

    def part_of(layer, h, b):
        return solved_all.at[layer, pl.ds(pl.multiple_of(h * half + b * step_rows, 8), step_rows)]

    def down_copy(b, sem, target):
        ref = part_of(y, core, b)
        return remote(ref, ref, bz_send.at[sem, b], bz_recv.at[b], target)

    def over_copy(b):
        ref = part_of(y, core, b)
        return remote(ref, ref, by_send.at[b], by_recv.at[b], across)

    def over_wait(b):
        ref = part_of(1 - y, core, b)
        remote(ref, ref, by_send.at[b], by_recv.at[b], across).wait_recv()

    def share_copy(turn, b):
        ref = part_of(layer_at(turn), core, b)
        return remote(ref, ref, bs_send.at[turn, b], bs_recv.at[turn, b], sibling)

    def share_wait(turn, b):
        ref = part_of(layer_at(turn), 1 - core, b)
        remote(ref, ref, bs_send.at[turn, b], bs_recv.at[turn, b], sibling).wait_recv()

    @pl.when(is_root)
    def _():
        for k in range(mine):
            for s in range(SPLIT):
                full_wait(k, s)
        eye = (
            lax.broadcasted_iota(jnp.int32, (TILE, TILE), 0)
            == lax.broadcasted_iota(jnp.int32, (TILE, TILE), 1)
        ).astype(F32)
        diagonal = jnp.zeros((TILE, TILE), F32)
        for i in range(strips):
            p = min(i, strips - 1 - i)
            start = 0 if i == p else (strips - p) * TILE
            lo, hi = i * TILE, (i + 1) * TILE
            strip = full[p, :, start:start + (strips - i) * TILE]
            diagonal = diagonal + strip[:, :TILE] * eye
            strip = strip * (1.0 / total_rows)
            hess[lo:hi, lo:] = strip
            if i < strips - 1:
                hess[hi:, lo:hi] = strip[:, TILE:].T
        trace = jnp.sum(jnp.sum(diagonal, axis=0, keepdims=True), axis=1, keepdims=True)
        damping = trace * (DAMPING / (total_rows * width))
        sums = jnp.zeros((1, width), F32)
        for i in range(strips):
            lo, hi = i * TILE, (i + 1) * TILE
            hess[lo:hi, lo:hi] = hess[lo:hi, lo:hi] + damping * eye
            block = hess[lo:hi, :]
            sums = sums + jnp.sum(jnp.abs(block), axis=0, keepdims=True)
            hess_high[lo:hi, :], hess_low[lo:hi, :] = halves(block)
        upper = jnp.max(sums, axis=1, keepdims=True)
        theta = (upper + damping) / 2.0
        delta = (upper - damping) / 2.0
        sigma = theta / delta

        for j in range(n // 2):
            at = pl.ds(j * depth, depth)
            source = (y * 0 + core) * (n // 2) + j
            waiting = remote(query.at[0], rhs.at[at], q_send.at[0], q_recv.at[j], sibling)

            @pl.when(source != me)
            def _():
                waiting.wait_recv()

            @pl.when(source == me)
            def _():
                pltpu.make_async_copy(query.at[0], rhs.at[at], q_local).wait()

        mine_rows = pl.ds(pl.multiple_of(core * half, 8), half)
        solved_all[y, mine_rows] = jnp.zeros((half, width), F32)
        direction[...] = rhs[...] / theta

        def step(_, rho):
            current = direction[...]
            solved_all[y, mine_rows] = solved_all[y, mine_rows] + current
            stacked[0:half], stacked[half:2 * half] = halves(current)
            dims = ((1,), (0,))
            wide = dot(stacked[0:2 * half], hess_high[...], dims)
            product = wide[:half] + (wide[half:] + dot(stacked[0:half], hess_low[...], dims))
            resid = rhs[...] - product
            rhs[...] = resid
            rho_new = 1.0 / (2.0 * sigma - rho)
            direction[...] = rho_new * rho * current + (2.0 * rho_new / delta) * resid
            return rho_new

        lax.fori_loop(0, ITERS - 1, step, 1.0 / sigma)
        solved_all[y, mine_rows] = solved_all[y, mine_rows] + direction[...]

    for b in range(PIECES):
        @pl.when(jnp.logical_not(is_root))
        def _():
            down_copy(b, 0, me).wait_recv()

        @pl.when(jnp.logical_and(z <= root, z > 0))
        def _():
            down_copy(b, 0, me - 4).start()

        @pl.when(jnp.logical_and(z >= root, z < chips - 1))
        def _():
            down_copy(b, 1, me + 4).start()

        over_copy(b).start()
        share_copy(1, b).start()
    for b in range(PIECES):
        over_wait(b)
        share_copy(0, b).start()
    for b in range(PIECES):
        share_wait(1, b)
        share_wait(0, b)

    scale = 1.0 / width ** 0.5
    block_rows = min(rows, 2 * TILE)
    count = 2 * half
    for turn in range(2):
        layer = layer_at(turn)
        stacked[0:count], stacked[count:2 * count] = halves(solved_all[layer])

        def score(b, _):
            at = pl.ds(pl.multiple_of(b * block_rows, block_rows), block_rows)
            dims = ((1,), (1,))
            wide = dot(stacked[...], high[turn, at], dims)
            value = wide[:count] + (wide[count:] + dot(stacked[0:count], low[turn, at], dims))
            if turn == 0:
                out[:, at] = value
            else:
                out[:, at] = (out[:, at] + value) * scale
            return 0

        lax.fori_loop(0, rows // block_rows, score, 0)

    for layer in range(layers):
        target, src, slot = query_copy(layer)

        @pl.when(target != me)
        def _():
            remote(src, slot, q_send.at[layer], q_recv.at[my_slot], target).wait_send()

    for k in range(mine):
        for turn in range(2):
            sib_copy(turn, k).wait_send()
        for s in range(SPLIT):
            y_copy(k, s).wait_send()

            @pl.when(z < root)
            def _():
                left_copy(k, s).wait_send()

            @pl.when(z > root)
            def _():
                right_copy(k, s).wait_send()

            @pl.when(is_root)
            def _():
                full_copy(k, s).wait_send()

    for b in range(PIECES):
        @pl.when(jnp.logical_and(z <= root, z > 0))
        def _():
            down_copy(b, 0, me - 4).wait_send()

        @pl.when(jnp.logical_and(z >= root, z < chips - 1))
        def _():
            down_copy(b, 1, me + 4).wait_send()

        over_copy(b).wait_send()
        share_copy(1, b).wait_send()
        share_copy(0, b).wait_send()


def shards(n, train_grads, query_grads):
    layers, rows, width = train_grads.shape
    depth = query_grads.shape[1]
    strips = width // TILE
    pairs, span = strips // 2, (strips + 1) * TILE
    mine = pairs // 2
    count = n * depth
    half = count // 2
    dma = pltpu.SemaphoreType.DMA
    return pl.pallas_call(
        functools.partial(kernel, n),
        out_shape=jax.ShapeDtypeStruct((count, rows), F32),
        in_specs=[
            pl.BlockSpec(memory_space=pl.ANY),
            pl.BlockSpec(memory_space=pltpu.VMEM),
        ],
        out_specs=pl.BlockSpec(memory_space=pltpu.VMEM),
        scratch_shapes=[
            pltpu.VMEM((layers, rows, width), F32),
            pltpu.VMEM((layers, rows, width), BF16),
            pltpu.VMEM((layers, rows, width), BF16),
            pltpu.VMEM((layers, pairs, TILE, span), F32),
            pltpu.VMEM((layers, mine, TILE, span), F32),
            pltpu.VMEM((layers, mine, TILE, span), F32),
            pltpu.VMEM((mine, TILE, span), F32),
            pltpu.VMEM((mine, TILE, span), F32),
            pltpu.VMEM((mine, TILE, span), F32),
            pltpu.VMEM((pairs, TILE, span), F32),
            pltpu.VMEM((width, width), F32),
            pltpu.VMEM((width, width), BF16),
            pltpu.VMEM((width, width), BF16),
            pltpu.VMEM((layers, count, width), F32),
            pltpu.VMEM((half, width), F32),
            pltpu.VMEM((half, width), F32),
            pltpu.VMEM((2 * count, width), BF16),
            dma((2,)), dma((layers,)), dma((n // 2,)), dma,
            dma((2, mine)), dma((2, mine)),
            dma((mine, SPLIT)), dma((mine, SPLIT)),
            dma((mine, SPLIT)), dma((mine, SPLIT)), dma((mine, SPLIT)),
            dma((mine, SPLIT)), dma((mine, SPLIT)),
            dma((2, PIECES)), dma((PIECES,)), dma((2, PIECES)),
            dma((PIECES,)), dma((PIECES,)), dma((2, PIECES)),
        ],
        compiler_params=pltpu.CompilerParams(
            collective_id=0, has_side_effects=True, vmem_limit_bytes=60 * 1024 * 1024
        ),
    )(train_grads, query_grads)


def solution(mesh):
    in_specs = (P(None, ("parts", "ex"), None), P(None, ("parts", "ex"), None))
    out_specs = P(None, ("parts", "ex"))
    return jax.shard_map(
        functools.partial(shards, mesh.shape["ex"]),
        mesh=mesh, in_specs=in_specs, out_specs=out_specs, check_vma=False,
    )
```

time: 394 us -> 85 us (0.22)
  waiting for transfers between devices: 208 us -> 0 us
  matrix products: 148 us -> 0 us
  Pallas kernels: 0 us -> 82.9 us
  between operations: 17.3 us -> 0.01 us
  other arithmetic: 13 us -> 0 us
    psum x1 -> x0, waiting for transfers between devices: 170 us -> none  [shards(): summed.append(lax.psum(payloads[layer], 'ex'))]
    dot_general x27 -> x0, matrix products: 148 us -> none  [the longest x24 103 us: step(): resid = resid - jnp.dot(direction, hess, precision=lax.Precision.HIGHEST)]
    pallas_call x0 -> x1, Pallas kernels: none -> 82.9 us  [shards(): pl.pallas_call(functools.partial(kernel, n), out_shape=jax.ShapeDtypeStru...]
    all_gather x1 -> x0, waiting for transfers between devices: 38.3 us -> none  [shards(): lax.all_gather(stacked, 'ex', axis=1, tiled=True)]
    reduce_sum x3 -> x0, other arithmetic: 11.1 us -> none  [the longest x1 7.24 us: precondition(): upper = jnp.max(jnp.sum(jnp.abs(hess), axis=1))]
  transfers between devices with their start and end apart: 2 -> 0, of which waited for: 2 -> 0; matrix products, arithmetic and copies ran while one was open for 0% -> 0% of each run, Pallas kernels for 0% -> 0%
where the time goes in v1:
time: 85 us; the launch traced here: 84.8 us
  Pallas kernels  82.9 us (98%)
  local copies, waits for them, and re-layouts  1.89 us (2%)
    pallas_call x1, Pallas kernels, shards(): pl.pallas_call(functools.partial(kernel, n), out_shape=jax.ShapeDtypeStru...  82.9 us
    unnamed x1, local copies, waits for them, and re-layouts  1.89 us

profile of v1, /device:TPU:27, one launch (start us, length us, event | category | flops | bytes accessed | tf_op | source)
XLA Modules:
  0.0 84.8 jit_solution(5663533713289915685)
XLA Ops:
  0.0 82.9 %shard_map.28 = f32[128,1024]{1,0:T(8,128)} custom-call(f32[2,1024,1024]{2,1,0:T(8,128)} %train.1, f32[2,8,1024]{2,1,0:T(8,128)} %query.1), custom_call_target="tpu_custom_call" | custom-call | tf_op jit(solution)/shard_map/pallas_call | solution.py:387
  82.9 1.9 %copy.4 = f32[128,1024]{1,0:T(8,128)} copy(f32[128,1024]{1,0:T(8,128)} %shard_map.28) | data formatting | bytes 1048576

commit v2 on v1

--- a/solution.py
+++ b/solution.py
@@ -10,8 +10,10 @@
 ITERS = 12
 DAMPING = 0.1
 TILE = 128
-SPLIT = 4
+SPLIT = 2
 PIECES = 4
+B_WINDOW = 4
+WINDOW = 4
 
 F32 = jnp.float32
 BF16 = jnp.bfloat16
@@ -40,7 +42,7 @@
 def kernel(
     n, train, query, out,
     rows_f32, high, low, part, acc, sib_buf, y_buf, left_buf, right_buf, full,
-    hess, hess_high, hess_low, solved_all, rhs, direction, stacked,
+    corner, sums, hess_high, hess_low, solved_all, rhs, direction, stacked,
     load_sem, q_send, q_recv, q_local, sib_send, sib_recv, y_send, y_recv, z_send, left_recv, right_recv,
     full_send, full_recv, bz_send, by_send, bs_send, bz_recv, by_recv, bs_recv,
 ):
@@ -48,8 +50,8 @@
     depth = query.shape[1]
     strips = width // TILE
     pairs = strips // 2
-    mine = pairs // 2
-    piece = TILE // SPLIT
+    share = TILE // 2
+    piece = share // SPLIT
     total_rows = rows * n
     half = depth * n // 2
     step_rows = half // PIECES
@@ -85,27 +87,27 @@
         return 0
 
     lax.fori_loop(1, n, greet, 0)
-    pl.semaphore_wait(barrier, n - 1)
 
     def query_copy(layer):
         target = root * 4 + layer * 2 + my_half
         slot = rhs.at[pl.ds(pl.multiple_of(my_slot * depth, 8), depth)]
         return target, query.at[layer], slot
 
-    for layer in range(layers):
-        target, src, slot = query_copy(layer)
-
-        @pl.when(target != me)
-        def _():
-            remote(src, slot, q_send.at[layer], q_recv.at[my_slot], target).start()
-
-        @pl.when(target == me)
-        def _():
-            pltpu.make_async_copy(src, slot, q_local).start()
+    def send_queries():
+        for layer in range(layers):
+            target, src, slot = query_copy(layer)
+
+            @pl.when(target != me)
+            def _():
+                remote(src, slot, q_send.at[layer], q_recv.at[my_slot], target).start()
+
+            @pl.when(target == me)
+            def _():
+                pltpu.make_async_copy(src, slot, q_local).start()
 
     def sib_copy(turn, k):
         return remote(
-            part.at[turn, 2 * k + 1 - core], sib_buf.at[turn, k],
+            part.at[turn, k, pl.ds(pl.multiple_of((1 - core) * share, 8), share)], sib_buf.at[turn, k],
             sib_send.at[turn, k], sib_recv.at[turn, k], sibling,
         )
 
@@ -122,23 +124,90 @@
         return remote(acc.at[1, k, sl], right_buf.at[k, sl], z_send.at[k, s], right_recv.at[k, s], me - 4)
 
     def full_copy(k, s):
-        src = full.at[2 * k + core, pl.ds(s * piece, piece)]
+        src = full.at[k, pl.ds(pl.multiple_of(core * share + s * piece, 8), piece)]
         return remote(src, src, full_send.at[k, s], full_recv.at[k, s], sibling)
 
     def full_wait(k, s):
-        src = full.at[2 * k + 1 - core, pl.ds(s * piece, piece)]
+        src = full.at[k, pl.ds(pl.multiple_of((1 - core) * share + s * piece, 8), piece)]
         remote(src, src, full_send.at[k, s], full_recv.at[k, s], sibling).wait_recv()
 
     def merge(turn, k):
         sib_copy(turn, k).wait_recv()
-        acc[turn, k] = part[turn, 2 * k + core] + sib_buf[turn, k]
+        acc[turn, k] = part[turn, k, pl.ds(pl.multiple_of(core * share, 8), share)] + sib_buf[turn, k]
 
         @pl.when(turn == 0)
         def _():
             for s in range(SPLIT):
-                y_copy(k, s).start()
-
-    def gram(turn, _):
+                if k * SPLIT + s < WINDOW:
+                    y_copy(k, s).start()
+
+    def pump(m):
+        if m < pairs * SPLIT - WINDOW:
+            y_copy(m // SPLIT, m % SPLIT).wait_send()
+            y_copy((m + WINDOW) // SPLIT, (m + WINDOW) % SPLIT).start()
+
+    eye = (
+        lax.broadcasted_iota(jnp.int32, (TILE, TILE), 0)
+        == lax.broadcasted_iota(jnp.int32, (TILE, TILE), 1)
+    ).astype(F32)
+
+    def assemble(k):
+        if k == 0:
+            sums[...] = jnp.zeros_like(sums)
+        column = 0
+        for i in (k, strips - 1 - k):
+            span = (strips - i) * TILE
+            lo, hi = i * TILE, (i + 1) * TILE
+            corner[i] = full[k, :, column:column + TILE] * (1.0 / total_rows)
+            if i < strips - 1:
+                strip = full[k, :, column + TILE:column + span] * (1.0 / total_rows)
+                turned = strip.T
+                hess_high[lo:hi, hi:], hess_low[lo:hi, hi:] = halves(strip)
+                hess_high[hi:, lo:hi], hess_low[hi:, lo:hi] = halves(turned)
+                sums[0:1, hi:] += jnp.sum(jnp.abs(strip), axis=0, keepdims=True)
+                sums[0:1, lo:hi] += jnp.sum(jnp.abs(turned), axis=0, keepdims=True)
+            column += span
+
+    from_left = jnp.logical_and(z > 0, z <= root)
+    from_right = jnp.logical_and(z < chips - 1, z >= root)
+    def chain(k):
+        for s in range(SPLIT):
+            sl = pl.ds(s * piece, piece)
+            y_copy(k, s).wait_recv()
+            pump(k * SPLIT + s)
+            acc[1, k, sl] = acc[1, k, sl] + y_buf[k, sl]
+
+            @pl.when(from_left)
+            def _():
+                left_copy(k, s).wait_recv()
+                acc[1, k, sl] = acc[1, k, sl] + left_buf[k, sl]
+
+            @pl.when(from_right)
+            def _():
+                right_copy(k, s).wait_recv()
+                acc[1, k, sl] = acc[1, k, sl] + right_buf[k, sl]
+
+            @pl.when(z < root)
+            def _():
+                left_copy(k, s).start()
+
+            @pl.when(z > root)
+            def _():
+                right_copy(k, s).start()
+
+            @pl.when(is_root)
+            def _():
+                full[k, pl.ds(pl.multiple_of(core * share + s * piece, 8), piece)] = acc[1, k, sl]
+                full_copy(k, s).start()
+
+    def gather(k):
+        @pl.when(is_root)
+        def _():
+            for s in range(SPLIT):
+                full_wait(k, s)
+            assemble(k)
+
+    def prepare(turn):
         load(turn).wait()
 
         def cut(b, _):
@@ -147,62 +216,52 @@
             return 0
 
         lax.fori_loop(0, rows // TILE, cut, 0)
+
+    def multiply(turn, p):
+        column = 0
+        for i in (p, strips - 1 - p):
+            span = (strips - i) * TILE
+            lo, hi = i * TILE, (i + 1) * TILE
+            left_high = high[turn, :, lo:hi]
+            left_low = low[turn, :, lo:hi]
+            right_high = high[turn, :, lo:]
+            right_low = low[turn, :, lo:]
+            dims = ((0,), (0,))
+            part[turn, p, :, column:column + span] = (
+                dot(left_high, right_low, dims) + dot(left_low, right_high, dims)
+            ) + dot(left_high, right_high, dims)
+            column += span
+
+    def gram(turn, _):
         for p in range(pairs):
-            column = 0
-            for i in (p, strips - 1 - p):
-                span = (strips - i) * TILE
-                lo, hi = i * TILE, (i + 1) * TILE
-                left_high = high[turn, :, lo:hi]
-                left_low = low[turn, :, lo:hi]
-                right_high = high[turn, :, lo:]
-                right_low = low[turn, :, lo:]
-                dims = ((0,), (0,))
-                part[turn, p, :, column:column + span] = (
-                    dot(left_high, right_low, dims) + dot(left_low, right_high, dims)
-                ) + dot(left_high, right_high, dims)
-                column += span
-
-            @pl.when(core != p % 2)
-            def _():
-                sib_copy(turn, p // 2).start()
-
-            if p >= 2 and p % 2 == 0:
-                merge(turn, p // 2 - 1)
-        merge(turn, mine - 1)
+            if p == 0:
+                @pl.when(turn == 1)
+                def _():
+                    prepare(1)
+                    multiply(1, 0)
+            else:
+                multiply(turn, p)
+            sib_copy(turn, p).start()
+            if p >= 1:
+                merge(turn, p - 1)
+            if p >= 2:
+                @pl.when(turn == 1)
+                def _():
+                    chain(p - 2)
+        merge(turn, pairs - 1)
         return 0
 
+    prepare(0)
+    multiply(0, 0)
+    pl.semaphore_wait(barrier, n - 1)
+    send_queries()
     lax.fori_loop(0, 2, gram, 0)
 
-    from_left = jnp.logical_and(z > 0, z <= root)
-    from_right = jnp.logical_and(z < chips - 1, z >= root)
-    for k in range(mine):
-        for s in range(SPLIT):
-            sl = pl.ds(s * piece, piece)
-            y_copy(k, s).wait_recv()
-            acc[1, k, sl] = acc[1, k, sl] + y_buf[k, sl]
-
-            @pl.when(from_left)
-            def _():
-                left_copy(k, s).wait_recv()
-                acc[1, k, sl] = acc[1, k, sl] + left_buf[k, sl]
-
-            @pl.when(from_right)
-            def _():
-                right_copy(k, s).wait_recv()
-                acc[1, k, sl] = acc[1, k, sl] + right_buf[k, sl]
-
-            @pl.when(z < root)
-            def _():
-                left_copy(k, s).start()
-
-            @pl.when(z > root)
-            def _():
-                right_copy(k, s).start()
-
-            @pl.when(is_root)
-            def _():
-                full[2 * k + core, sl] = acc[1, k, sl]
-                full_copy(k, s).start()
+    gather(0)
+    for k in range(pairs - 2, pairs):
+        chain(k)
+        gather(k - 1)
+    gather(pairs - 1)
 
     def part_of(layer, h, b):
         return solved_all.at[layer, pl.ds(pl.multiple_of(h * half + b * step_rows, 8), step_rows)]
@@ -229,34 +288,17 @@
 
     @pl.when(is_root)
     def _():
-        for k in range(mine):
-            for s in range(SPLIT):
-                full_wait(k, s)
-        eye = (
-            lax.broadcasted_iota(jnp.int32, (TILE, TILE), 0)
-            == lax.broadcasted_iota(jnp.int32, (TILE, TILE), 1)
-        ).astype(F32)
         diagonal = jnp.zeros((TILE, TILE), F32)
         for i in range(strips):
-            p = min(i, strips - 1 - i)
-            start = 0 if i == p else (strips - p) * TILE
-            lo, hi = i * TILE, (i + 1) * TILE
-            strip = full[p, :, start:start + (strips - i) * TILE]
-            diagonal = diagonal + strip[:, :TILE] * eye
-            strip = strip * (1.0 / total_rows)
-            hess[lo:hi, lo:] = strip
-            if i < strips - 1:
-                hess[hi:, lo:hi] = strip[:, TILE:].T
+            diagonal = diagonal + corner[i] * eye
         trace = jnp.sum(jnp.sum(diagonal, axis=0, keepdims=True), axis=1, keepdims=True)
-        damping = trace * (DAMPING / (total_rows * width))
-        sums = jnp.zeros((1, width), F32)
+        damping = trace * (DAMPING / width)
         for i in range(strips):
             lo, hi = i * TILE, (i + 1) * TILE
-            hess[lo:hi, lo:hi] = hess[lo:hi, lo:hi] + damping * eye
-            block = hess[lo:hi, :]
-            sums = sums + jnp.sum(jnp.abs(block), axis=0, keepdims=True)
-            hess_high[lo:hi, :], hess_low[lo:hi, :] = halves(block)
-        upper = jnp.max(sums, axis=1, keepdims=True)
+            block = corner[i] + damping * eye
+            sums[0:1, lo:hi] += jnp.sum(jnp.abs(block), axis=0, keepdims=True)
+            hess_high[lo:hi, lo:hi], hess_low[lo:hi, lo:hi] = halves(block)
+        upper = jnp.max(sums[0:1], axis=1, keepdims=True)
         theta = (upper + damping) / 2.0
         delta = (upper - damping) / 2.0
         sigma = theta / delta
@@ -294,11 +336,26 @@
         lax.fori_loop(0, ITERS - 1, step, 1.0 / sigma)
         solved_all[y, mine_rows] = solved_all[y, mine_rows] + direction[...]
 
+    def sent(b):
+        @pl.when(jnp.logical_and(z <= root, z > 0))
+        def _():
+            down_copy(b, 0, me - 4).wait_send()
+
+        @pl.when(jnp.logical_and(z >= root, z < chips - 1))
+        def _():
+            down_copy(b, 1, me + 4).wait_send()
+
+        over_copy(b).wait_send()
+        share_copy(1, b).wait_send()
+
     for b in range(PIECES):
         @pl.when(jnp.logical_not(is_root))
         def _():
             down_copy(b, 0, me).wait_recv()
 
+        if b >= B_WINDOW:
+            sent(b - B_WINDOW)
+
         @pl.when(jnp.logical_and(z <= root, z > 0))
         def _():
             down_copy(b, 0, me - 4).start()
@@ -309,9 +366,11 @@
 
         over_copy(b).start()
         share_copy(1, b).start()
-    for b in range(PIECES):
-        over_wait(b)
-        share_copy(0, b).start()
+        if b >= 1:
+            over_wait(b - 1)
+            share_copy(0, b - 1).start()
+    over_wait(PIECES - 1)
+    share_copy(0, PIECES - 1).start()
     for b in range(PIECES):
         share_wait(1, b)
         share_wait(0, b)
@@ -343,11 +402,12 @@
         def _():
             remote(src, slot, q_send.at[layer], q_recv.at[my_slot], target).wait_send()
 
-    for k in range(mine):
+    for k in range(pairs):
         for turn in range(2):
             sib_copy(turn, k).wait_send()
         for s in range(SPLIT):
-            y_copy(k, s).wait_send()
+            if k * SPLIT + s >= pairs * SPLIT - WINDOW:
+                y_copy(k, s).wait_send()
 
             @pl.when(z < root)
             def _():
@@ -361,17 +421,9 @@
             def _():
                 full_copy(k, s).wait_send()
 
+    for b in range(PIECES - B_WINDOW, PIECES):
+        sent(b)
     for b in range(PIECES):
-        @pl.when(jnp.logical_and(z <= root, z > 0))
-        def _():
-            down_copy(b, 0, me - 4).wait_send()
-
-        @pl.when(jnp.logical_and(z >= root, z < chips - 1))
-        def _():
-            down_copy(b, 1, me + 4).wait_send()
-
-        over_copy(b).wait_send()
-        share_copy(1, b).wait_send()
         share_copy(0, b).wait_send()
 
 
@@ -380,7 +432,7 @@
     depth = query_grads.shape[1]
     strips = width // TILE
     pairs, span = strips // 2, (strips + 1) * TILE
-    mine = pairs // 2
+    share = TILE // 2
     count = n * depth
     half = count // 2
     dma = pltpu.SemaphoreType.DMA
@@ -397,13 +449,14 @@
             pltpu.VMEM((layers, rows, width), BF16),
             pltpu.VMEM((layers, rows, width), BF16),
             pltpu.VMEM((layers, pairs, TILE, span), F32),
-            pltpu.VMEM((layers, mine, TILE, span), F32),
-            pltpu.VMEM((layers, mine, TILE, span), F32),
-            pltpu.VMEM((mine, TILE, span), F32),
-            pltpu.VMEM((mine, TILE, span), F32),
-            pltpu.VMEM((mine, TILE, span), F32),
+            pltpu.VMEM((layers, pairs, share, span), F32),
+            pltpu.VMEM((layers, pairs, share, span), F32),
+            pltpu.VMEM((pairs, share, span), F32),
+            pltpu.VMEM((pairs, share, span), F32),
+            pltpu.VMEM((pairs, share, span), F32),
             pltpu.VMEM((pairs, TILE, span), F32),
-            pltpu.VMEM((width, width), F32),
+            pltpu.VMEM((strips, TILE, TILE), F32),
+            pltpu.VMEM((8, width), F32),
             pltpu.VMEM((width, width), BF16),
             pltpu.VMEM((width, width), BF16),
             pltpu.VMEM((layers, count, width), F32),
@@ -411,10 +464,10 @@
             pltpu.VMEM((half, width), F32),
             pltpu.VMEM((2 * count, width), BF16),
             dma((2,)), dma((layers,)), dma((n // 2,)), dma,
-            dma((2, mine)), dma((2, mine)),
-            dma((mine, SPLIT)), dma((mine, SPLIT)),
-            dma((mine, SPLIT)), dma((mine, SPLIT)), dma((mine, SPLIT)),
-            dma((mine, SPLIT)), dma((mine, SPLIT)),
+            dma((2, pairs)), dma((2, pairs)),
+            dma((pairs, SPLIT)), dma((pairs, SPLIT)),
+            dma((pairs, SPLIT)), dma((pairs, SPLIT)), dma((pairs, SPLIT)),
+            dma((pairs, SPLIT)), dma((pairs, SPLIT)),
             dma((2, PIECES)), dma((PIECES,)), dma((2, PIECES)),
             dma((PIECES,)), dma((PIECES,)), dma((2, PIECES)),
         ],

time: 85 us -> 82.8 us (0.974)
  Pallas kernels: 82.9 us -> 80.3 us
    pallas_call x1, Pallas kernels: 82.9 us -> 80.3 us  [shards(): pl.pallas_call(functools.partial(kernel, n), out_shape=jax.ShapeDtypeStru...]
where the time goes in v2:
time: 82.8 us; the launch traced here: 82.2 us
  Pallas kernels  80.3 us (97%)
  local copies, waits for them, and re-layouts  1.89 us (2%)
    pallas_call x1, Pallas kernels, shards(): pl.pallas_call(functools.partial(kernel, n), out_shape=jax.ShapeDtypeStru...  80.3 us
    unnamed x1, local copies, waits for them, and re-layouts  1.89 us

profile of v2, /device:TPU:27, one launch (start us, length us, event | category | flops | bytes accessed | tf_op | source)
XLA Modules:
  0.0 82.2 jit_solution(16248310445105538567)
XLA Ops:
  0.0 80.3 %shard_map.28 = f32[128,1024]{1,0:T(8,128)} custom-call(f32[2,1024,1024]{2,1,0:T(8,128)} %train.1, f32[2,8,1024]{2,1,0:T(8,128)} %query.1), custom_call_target="tpu_custom_call" | custom-call | tf_op jit(solution)/shard_map/pallas_call | solution.py:439
  80.3 1.9 %copy.4 = f32[128,1024]{1,0:T(8,128)} copy(f32[128,1024]{1,0:T(8,128)} %shard_map.28) | data formatting | bytes 1048576

commit v3 on v2

--- a/solution.py
+++ b/solution.py
@@ -369,16 +369,15 @@
         if b >= 1:
             over_wait(b - 1)
             share_copy(0, b - 1).start()
-    over_wait(PIECES - 1)
-    share_copy(0, PIECES - 1).start()
-    for b in range(PIECES):
-        share_wait(1, b)
-        share_wait(0, b)
-
     scale = 1.0 / width ** 0.5
     block_rows = min(rows, 2 * TILE)
     count = 2 * half
-    for turn in range(2):
+    for turn in (1, 0):
+        if turn == 0:
+            over_wait(PIECES - 1)
+            share_copy(0, PIECES - 1).start()
+        for b in range(PIECES):
+            share_wait(turn, b)
         layer = layer_at(turn)
         stacked[0:count], stacked[count:2 * count] = halves(solved_all[layer])
 
@@ -387,7 +386,7 @@
             dims = ((1,), (1,))
             wide = dot(stacked[...], high[turn, at], dims)
             value = wide[:count] + (wide[count:] + dot(stacked[0:count], low[turn, at], dims))
-            if turn == 0:
+            if turn == 1:
                 out[:, at] = value
             else:
                 out[:, at] = (out[:, at] + value) * scale

time: 82.8 us -> 81.5 us (0.984)
  Pallas kernels: 80.3 us -> 79.4 us
    pallas_call x1, Pallas kernels: 80.3 us -> 79.4 us  [shards(): pl.pallas_call(functools.partial(kernel, n), out_shape=jax.ShapeDtypeStru...]
where the time goes in v3:
time: 81.5 us; the launch traced here: 81.3 us
  Pallas kernels  79.4 us (97%)
  local copies, waits for them, and re-layouts  1.89 us (2%)
    pallas_call x1, Pallas kernels, shards(): pl.pallas_call(functools.partial(kernel, n), out_shape=jax.ShapeDtypeStru...  79.4 us
    unnamed x1, local copies, waits for them, and re-layouts  1.89 us

profile of v3, /device:TPU:27, one launch (start us, length us, event | category | flops | bytes accessed | tf_op | source)
XLA Modules:
  0.0 81.3 jit_solution(3953764846841733474)
XLA Ops:
  0.0 79.4 %shard_map.28 = f32[128,1024]{1,0:T(8,128)} custom-call(f32[2,1024,1024]{2,1,0:T(8,128)} %train.1, f32[2,8,1024]{2,1,0:T(8,128)} %query.1), custom_call_target="tpu_custom_call" | custom-call | tf_op jit(solution)/shard_map/pallas_call | solution.py:438
  79.4 1.9 %copy.4 = f32[128,1024]{1,0:T(8,128)} copy(f32[128,1024]{1,0:T(8,128)} %shard_map.28) | data formatting | bytes 1048576
